TPU v7x, 32 devices: a whole 2x2x4 slice. The times are simulated.
32 devices in a mesh: row: 8 (over z, y), col: 4 (over x, core).
Axes of the slice: x: 2, y: 2, z: 4, core: 2. Of those that a mesh axis runs over, the one named last changes fastest.
Arguments:
- features: bfloat16 [4096, 1024], P(('row', 'col')), may hold values from -12 to 12
- tile_values: bfloat16 [8, 4, 24, 128, 128], P('row', 'col'), as said below
- tile_rows: int32 [8, 4, 24], P('row', 'col'), may hold values from 0 to 3
- tile_cols: int32 [8, 4, 24], P('row', 'col'), may hold values from 0 to 7
- tile_count: int32 [8, 4], P('row', 'col'), may hold values from 3 to 24, as said below
Outputs:
- smoothed: bfloat16 [4096, 1024], P(('row', 'col'))
Inputs may be any that keep to these rules, and one draw needn't show every extreme that they name: `tile_count`: live slots of one device sit at distinct tile positions; in every grid row exactly one device has all 24 slots live. `tile_values`: edge weights are zero or positive.
All inputs are finite; a program needn't handle non-finite values.
Results may differ from a plain program's by a relative error of at most 0.0075.
Values may be sent and summed in bfloat16 or wider, within the bound.
A program may use at most 64 MiB of HBM per device.

v0:
```python
import jax
import jax.numpy as jnp
from jax import lax
from jax.sharding import PartitionSpec as P

ITERS = 2


retain_share = 0.9
restart_share = 0.1


def body(features, tile_values, tile_rows, tile_cols, tile_count):
    shard_rows, feature_width = features.shape
    capacity = tile_values.shape[2]
    tile_size = tile_values.shape[3]
    tile_set = tile_values.reshape(capacity, tile_size, tile_size)
    row_ids = tile_rows.reshape(capacity)
    col_ids = tile_cols.reshape(capacity)
    live_count = tile_count.reshape(1)
    block_rows = shard_rows * lax.axis_size("col") // tile_size
    block_cols = shard_rows * lax.axis_size("row") // tile_size
    group_size = 8
    row_range = jnp.arange(block_rows, dtype=jnp.int32)
    is_live = jnp.arange(capacity, dtype=jnp.int32) < live_count[0]
    row_hot = ((row_ids[None, :] == row_range[:, None]) & is_live[None, :]).astype(jnp.float32)
    row_sums = jnp.sum(tile_set, axis=2, dtype=jnp.float32)
    degree_part = jnp.einsum(
        "rt,ti->ri", row_hot, row_sums, precision=lax.Precision.HIGHEST
    ).reshape(block_rows * tile_size)
    degree = 1.0 + lax.psum_scatter(degree_part, "col", scatter_dimension=0, tiled=True)

    def contribute(column_blocks, pool_tiles, pool_rows, pool_cols, picked):
        chosen = jnp.take(pool_tiles, picked, axis=0)
        needed = jnp.take(column_blocks, jnp.take(pool_cols, picked), axis=0)
        product = jnp.einsum("tij,tjf->tif", chosen, needed, preferred_element_type=jnp.float32)
        return (product, jnp.take(pool_rows, picked))

    source = features.astype(jnp.float32)
    current = features
    for iteration in range(ITERS):
        gathered = lax.all_gather(current, "row", axis=0, tiled=True)
        products_column_blocks = gathered.reshape(block_cols, tile_size, feature_width)
        zeroes = jnp.zeros((block_rows, tile_size, feature_width), jnp.float32)

        def own_turn(step_index, total):
            picked = step_index * group_size + jnp.arange(group_size, dtype=jnp.int32)
            usable = picked < live_count[0]
            product, targets = contribute(
                products_column_blocks, tile_set, row_ids, col_ids, picked
            )
            placed = jnp.where(usable, targets, block_rows)
            return total.at[placed].add(product, mode="drop")

        turn_count = capacity // group_size
        partial_value = lax.fori_loop(0, turn_count, own_turn, zeroes)
        summed = lax.psum_scatter(
            partial_value.reshape(block_rows * tile_size, feature_width).astype(jnp.bfloat16),
            "col",
            scatter_dimension=0,
            tiled=True,
        ).astype(jnp.float32)
        current = (
            retain_share * (summed + current.astype(jnp.float32)) / degree[:, None]
            + restart_share * source
        ).astype(jnp.bfloat16)
    return current


def solution(mesh):
    return jax.shard_map(
        body,
        mesh=mesh,
        in_specs=(
            P(("row", "col"), None),
            P("row", "col", None, None, None),
            P("row", "col", None),
            P("row", "col", None),
            P("row", "col"),
        ),
        out_specs=P(("row", "col"), None),
        check_vma=False,
    )
```

profile of v0, /device:TPU:0, one launch (start us, length us, event | category | flops | bytes accessed | tf_op | source)
XLA Modules:
  0.0 269.6 jit_solution(11322371293256857345)
XLA Ops:
  7.3 54.2 %all-gather.3.cloned.1.call-done = bf16[1024,1024]{1,0:T(8,128)(2,1)} async-done(((bf16[128,1024]{1,0:T(8,128)(2,1)}), bf16[1024,1024]{1,0:T(8,128)(2,1)}) %all-gather.3.cloned.1.call-update) | async-done | bytes 2097168 | tf_op jit(solution)/shard_map/all_gather | solution.py:42
  61.8 49.0 %while.26 = (s32[]{:T(128)}, f32[4,128,1024]{2,1,0:T(8,128)S(1)}, s32[1,1]{1,0:T(1,128)}, s32[24]{0:T(128)S(1)}, bf16[24,128,128]{2,1,0:T(8,128)(2,1)S(1)}, /*in...) while((s32[]{:T(128)}, f32[4,128,1024]{2,1,0:T(8,128)S(1)}, s32[1,1]{1,0:T(1,128)}, ...), condition=%wide.region_2.6_spmd, body=%wide.region_0.5_spmd.sunk | while | flops 270665984 | bytes 23863960 | solution.py:56
  64.4 3.6 %gather_fusion.2 = bf16[8,128,1024]{2,1,0:T(8,128)(2,1)} fusion(bf16[8,128,1024]{2,1,0:T(8,128)(2,1)} %get-tuple-element.414, s32[1024]{0:T(1024)S(1)} %pad_clamp_fusion.9), kind=kCustom, calls=%fused_computation.2.clone.clone.1 | custom fusion | bytes 4194336 | tf_op jit(solution)/shard_map/while/body/eval_jaxpr/jit(_take)/gather | solution.py:35
  68.0 4.3 %fusion.35 = f32[8,128,1024]{2,1,0:T(8,128)} fusion(bf16[8,128,1024]{2,1,0:T(8,128)(2,1)} %gather_fusion.2, pred[8]{0:T(512)(128)(4,1)S(1)} %get-tuple-element.378, bf16[8,128,128]{2,1,0:T(8,128)(2,1)S(1)} %gather_fusion.3, pred[8]{0:T(512)(128)(4,1)S(1)} %get-tuple-element.379), kind=kOutput, calls=%fused_computation.10.clone.1 | convolution fusion | flops 269615104 | bytes 6553616 | tf_op jit(solution)/shard_map/while/body/eval_jaxpr/tij,tjf->tif/dot_general | solution.py:36
  72.3 5.8 %scatter_fusion = f32[4,128,1024]{2,1,0:T(8,128)S(1)} fusion(f32[4,128,1024]{2,1,0:T(8,128)S(1)} %get-tuple-element.400, s32[8]{0:T(128)S(1)} %compare_select_fusion.15, f32[8,128,1024]{2,1,0:T(8,128)} %fusion.35), kind=kCustom, calls=%fused_computation.8.clone.1 | custom fusion | flops 1048576 | bytes 12582944 | tf_op jit(solution)/shard_map/while/body/eval_jaxpr/scatter-add | solution.py:53
  80.8 3.6 %gather_fusion.2 = bf16[8,128,1024]{2,1,0:T(8,128)(2,1)} fusion(bf16[8,128,1024]{2,1,0:T(8,128)(2,1)} %get-tuple-element.414, s32[1024]{0:T(1024)S(1)} %pad_clamp_fusion.9), kind=kCustom, calls=%fused_computation.2.clone.clone.1 | custom fusion | bytes 4194336 | tf_op jit(solution)/shard_map/while/body/eval_jaxpr/jit(_take)/gather | solution.py:35
  84.4 4.3 %fusion.35 = f32[8,128,1024]{2,1,0:T(8,128)} fusion(bf16[8,128,1024]{2,1,0:T(8,128)(2,1)} %gather_fusion.2, pred[8]{0:T(512)(128)(4,1)S(1)} %get-tuple-element.378, bf16[8,128,128]{2,1,0:T(8,128)(2,1)S(1)} %gather_fusion.3, pred[8]{0:T(512)(128)(4,1)S(1)} %get-tuple-element.379), kind=kOutput, calls=%fused_computation.10.clone.1 | convolution fusion | flops 269615104 | bytes 6553616 | tf_op jit(solution)/shard_map/while/body/eval_jaxpr/tij,tjf->tif/dot_general | solution.py:36
  88.7 5.8 %scatter_fusion = f32[4,128,1024]{2,1,0:T(8,128)S(1)} fusion(f32[4,128,1024]{2,1,0:T(8,128)S(1)} %get-tuple-element.400, s32[8]{0:T(128)S(1)} %compare_select_fusion.15, f32[8,128,1024]{2,1,0:T(8,128)} %fusion.35), kind=kCustom, calls=%fused_computation.8.clone.1 | custom fusion | flops 1048576 | bytes 12582944 | tf_op jit(solution)/shard_map/while/body/eval_jaxpr/scatter-add | solution.py:53
  97.1 3.6 %gather_fusion.2 = bf16[8,128,1024]{2,1,0:T(8,128)(2,1)} fusion(bf16[8,128,1024]{2,1,0:T(8,128)(2,1)} %get-tuple-element.414, s32[1024]{0:T(1024)S(1)} %pad_clamp_fusion.9), kind=kCustom, calls=%fused_computation.2.clone.clone.1 | custom fusion | bytes 4194336 | tf_op jit(solution)/shard_map/while/body/eval_jaxpr/jit(_take)/gather | solution.py:35
  100.7 4.3 %fusion.35 = f32[8,128,1024]{2,1,0:T(8,128)} fusion(bf16[8,128,1024]{2,1,0:T(8,128)(2,1)} %gather_fusion.2, pred[8]{0:T(512)(128)(4,1)S(1)} %get-tuple-element.378, bf16[8,128,128]{2,1,0:T(8,128)(2,1)S(1)} %gather_fusion.3, pred[8]{0:T(512)(128)(4,1)S(1)} %get-tuple-element.379), kind=kOutput, calls=%fused_computation.10.clone.1 | convolution fusion | flops 269615104 | bytes 6553616 | tf_op jit(solution)/shard_map/while/body/eval_jaxpr/tij,tjf->tif/dot_general | solution.py:36
  105.0 5.8 %scatter_fusion = f32[4,128,1024]{2,1,0:T(8,128)S(1)} fusion(f32[4,128,1024]{2,1,0:T(8,128)S(1)} %get-tuple-element.400, s32[8]{0:T(128)S(1)} %compare_select_fusion.15, f32[8,128,1024]{2,1,0:T(8,128)} %fusion.35), kind=kCustom, calls=%fused_computation.8.clone.1 | custom fusion | flops 1048576 | bytes 12582944 | tf_op jit(solution)/shard_map/while/body/eval_jaxpr/scatter-add | solution.py:53
  114.4 5.6 %all-reduce = f32[512]{0:T(512)S(1)} all-reduce(f32[512]{0:T(512)S(1)} %convolution_bitcast_fusion), channel_id=3, replica_groups=mesh['row'=8,'col'=4] {'col'}, use_global_device_ids=true, to_apply=%region_5.9.clone | all-reduce | flops 512 | bytes 4096
  120.1 15.4 %reduce-scatter.3.cloned.1.call-done = bf16[128,1024]{1,0:T(8,128)(2,1)} async-done(((bf16[512,1024]{1,0:T(8,128)(2,1)}), bf16[128,1024]{1,0:T(8,128)(2,1)}) %reduce-scatter.3.cloned.1.call-update) | async-done | bytes 262160 | tf_op jit(solution)/shard_map/reduce_scatter | solution.py:57
  137.4 49.8 %all-gather.5.cloned.1.call-done = bf16[1024,1024]{1,0:T(8,128)(2,1)} async-done(((bf16[128,1024]{1,0:T(8,128)(2,1)}), bf16[1024,1024]{1,0:T(8,128)(2,1)}) %all-gather.5.cloned.1.call-update) | async-done | bytes 2097168 | tf_op jit(solution)/shard_map/all_gather | solution.py:42
  187.5 49.0 %while.27 = (s32[]{:T(128)}, f32[4,128,1024]{2,1,0:T(8,128)S(1)}, s32[1,1]{1,0:T(1,128)}, s32[24]{0:T(128)S(1)}, bf16[24,128,128]{2,1,0:T(8,128)(2,1)S(1)}, /*in...) while((s32[]{:T(128)}, f32[4,128,1024]{2,1,0:T(8,128)S(1)}, s32[1,1]{1,0:T(1,128)}, ...), condition=%wide.region_8.12_spmd, body=%wide.region_6.0_spmd.sunk | while | flops 270665984 | bytes 23863960 | solution.py:56
  190.1 3.6 %gather_fusion.6 = bf16[8,128,1024]{2,1,0:T(8,128)(2,1)} fusion(bf16[8,128,1024]{2,1,0:T(8,128)(2,1)} %get-tuple-element.441, s32[1024]{0:T(1024)S(1)} %pad_clamp_fusion.11), kind=kCustom, calls=%fused_computation.7.clone.clone.1 | custom fusion | bytes 4194336 | tf_op jit(solution)/shard_map/while/body/eval_jaxpr/jit(_take)/gather | solution.py:35
  193.7 4.3 %fusion.38 = f32[8,128,1024]{2,1,0:T(8,128)} fusion(bf16[8,128,1024]{2,1,0:T(8,128)(2,1)} %gather_fusion.6, pred[8]{0:T(512)(128)(4,1)S(1)} %get-tuple-element.388, bf16[8,128,128]{2,1,0:T(8,128)(2,1)S(1)} %gather_fusion.7, pred[8]{0:T(512)(128)(4,1)S(1)} %get-tuple-element.389), kind=kOutput, calls=%fused_computation.27.clone.1 | convolution fusion | flops 269615104 | bytes 6553616 | tf_op jit(solution)/shard_map/while/body/eval_jaxpr/tij,tjf->tif/dot_general | solution.py:36
  198.0 5.8 %scatter_fusion.1 = f32[4,128,1024]{2,1,0:T(8,128)S(1)} fusion(f32[4,128,1024]{2,1,0:T(8,128)S(1)} %get-tuple-element.427, s32[8]{0:T(128)S(1)} %compare_select_fusion.17, f32[8,128,1024]{2,1,0:T(8,128)} %fusion.38), kind=kCustom, calls=%fused_computation.9.clone.1 | custom fusion | flops 1048576 | bytes 12582944 | tf_op jit(solution)/shard_map/while/body/eval_jaxpr/scatter-add | solution.py:53
  210.0 4.3 %fusion.38 = f32[8,128,1024]{2,1,0:T(8,128)} fusion(bf16[8,128,1024]{2,1,0:T(8,128)(2,1)} %gather_fusion.6, pred[8]{0:T(512)(128)(4,1)S(1)} %get-tuple-element.388, bf16[8,128,128]{2,1,0:T(8,128)(2,1)S(1)} %gather_fusion.7, pred[8]{0:T(512)(128)(4,1)S(1)} %get-tuple-element.389), kind=kOutput, calls=%fused_computation.27.clone.1 | convolution fusion | flops 269615104 | bytes 6553616 | tf_op jit(solution)/shard_map/while/body/eval_jaxpr/tij,tjf->tif/dot_general | solution.py:36
  214.3 5.8 %scatter_fusion.1 = f32[4,128,1024]{2,1,0:T(8,128)S(1)} fusion(f32[4,128,1024]{2,1,0:T(8,128)S(1)} %get-tuple-element.427, s32[8]{0:T(128)S(1)} %compare_select_fusion.17, f32[8,128,1024]{2,1,0:T(8,128)} %fusion.38), kind=kCustom, calls=%fused_computation.9.clone.1 | custom fusion | flops 1048576 | bytes 12582944 | tf_op jit(solution)/shard_map/while/body/eval_jaxpr/scatter-add | solution.py:53
  222.8 3.6 %gather_fusion.6 = bf16[8,128,1024]{2,1,0:T(8,128)(2,1)} fusion(bf16[8,128,1024]{2,1,0:T(8,128)(2,1)} %get-tuple-element.441, s32[1024]{0:T(1024)S(1)} %pad_clamp_fusion.11), kind=kCustom, calls=%fused_computation.7.clone.clone.1 | custom fusion | bytes 4194336 | tf_op jit(solution)/shard_map/while/body/eval_jaxpr/jit(_take)/gather | solution.py:35
  226.4 4.3 %fusion.38 = f32[8,128,1024]{2,1,0:T(8,128)} fusion(bf16[8,128,1024]{2,1,0:T(8,128)(2,1)} %gather_fusion.6, pred[8]{0:T(512)(128)(4,1)S(1)} %get-tuple-element.388, bf16[8,128,128]{2,1,0:T(8,128)(2,1)S(1)} %gather_fusion.7, pred[8]{0:T(512)(128)(4,1)S(1)} %get-tuple-element.389), kind=kOutput, calls=%fused_computation.27.clone.1 | convolution fusion | flops 269615104 | bytes 6553616 | tf_op jit(solution)/shard_map/while/body/eval_jaxpr/tij,tjf->tif/dot_general | solution.py:36
  230.7 5.8 %scatter_fusion.1 = f32[4,128,1024]{2,1,0:T(8,128)S(1)} fusion(f32[4,128,1024]{2,1,0:T(8,128)S(1)} %get-tuple-element.427, s32[8]{0:T(128)S(1)} %compare_select_fusion.17, f32[8,128,1024]{2,1,0:T(8,128)} %fusion.38), kind=kCustom, calls=%fused_computation.9.clone.1 | custom fusion | flops 1048576 | bytes 12582944 | tf_op jit(solution)/shard_map/while/body/eval_jaxpr/scatter-add | solution.py:53
  237.6 23.5 %reduce-scatter.5.cloned.1.call-done = bf16[128,1024]{1,0:T(8,128)(2,1)} async-done(((bf16[512,1024]{1,0:T(8,128)(2,1)}), bf16[128,1024]{1,0:T(8,128)(2,1)}) %reduce-scatter.5.cloned.1.call-update) | async-done | bytes 262160 | tf_op jit(solution)/shard_map/reduce_scatter | solution.py:57
  (80 shorter events, 27.5 us)
Async XLA Ops:
  6.5 55.2 %copy-start.2 = (bf16[1,1,24,128,128]{4,3,2,1,0:T(8,128)(2,1)S(1)}, bf16[1,1,24,128,128]{4,3,2,1,0:T(8,128)(2,1)}, u32[]{:S(2)}) copy-start(bf16[1,1,24,128,128]{4,3,2,1,0:T(8,128)(2,1)} %param.16) | copy-start | bytes 2359300
  6.5 55.2 %copy-start.1 = (s32[1,1,24]{2,1,0:T(1,128)S(1)}, s32[1,1,24]{2,1,0:T(1,128)}, u32[]{:S(2)}) copy-start(s32[1,1,24]{2,1,0:T(1,128)} %param.18) | copy-start | bytes 292
  6.5 55.2 %copy-start = (s32[1,1,24]{2,1,0:T(1,128)S(1)}, s32[1,1,24]{2,1,0:T(1,128)}, u32[]{:S(2)}) copy-start(s32[1,1,24]{2,1,0:T(1,128)} %param.17) | copy-start | bytes 292
  6.5 55.0 %all-gather.3.cloned.1.call-start = ((), (), s32[]{:S(2)}) async-start(), calls=%async_computation.2 | async-start | bytes 2359296 | tf_op jit(solution)/shard_map/all_gather | solution.py:42
  7.3 128.2 %reduce-scatter.3.cloned.1.call-start = ((), (), s32[]{:S(2)}) async-start(), calls=%async_computation.3 | async-start | bytes 1310720 | tf_op jit(solution)/shard_map/reduce_scatter | solution.py:57
  110.8 1.9 copy-start.5
  110.8 24.7 %copy-start.3 = (bf16[128,1024]{1,0:T(8,128)(2,1)S(1)}, bf16[128,1024]{1,0:T(8,128)(2,1)}, u32[]{:S(2)}) copy-start(bf16[128,1024]{1,0:T(8,128)(2,1)} %param.15) | copy-start | bytes 786436
  112.0 75.2 %all-gather.5.cloned.1.call-start = ((), (), s32[]{:S(2)}) async-start(), calls=%async_computation.4 | async-start | bytes 2359296 | tf_op jit(solution)/shard_map/all_gather | solution.py:42
  137.4 123.8 %reduce-scatter.5.cloned.1.call-start = ((), (), s32[]{:S(2)}) async-start(), calls=%async_computation.5 | async-start | bytes 1310720 | tf_op jit(solution)/shard_map/reduce_scatter | solution.py:57
  236.5 24.7 %copy-start.4 = (bf16[128,1024]{1,0:T(8,128)(2,1)S(1)}, bf16[128,1024]{1,0:T(8,128)(2,1)}, u32[]{:S(2)}) copy-start(bf16[128,1024]{1,0:T(8,128)(2,1)} %fusion.18) | copy-start | bytes 786436
Sparse Core Ops, SparseCore 0:
  9.5 51.9 all-gather.2
  112.1 23.3 reduce-scatter.2
  137.9 49.3 all-gather.4
  237.8 23.3 reduce-scatter.4
where the time goes:
time: 271 us; the launch traced here: 270 us
  waiting for transfers between devices  144 us (53%)
  other arithmetic  45.2 us (17%)
  local copies, waits for them, and re-layouts  34.1 us (13%)
  matrix products  25.9 us (10%)
  between operations  14.5 us (5%)
  blocking collectives  5.64 us (2%)
    all_gather x2, waiting for transfers between devices, body(): gathered = lax.all_gather(current, 'row', axis=0, tiled=True)  104 us
    reduce_scatter x2, waiting for transfers between devices, body(): lax.psum_scatter(partial_value.reshape(block_rows * tile_size, feature_wi...  38.9 us
    scatter-add x6, other arithmetic, own_turn(): return total.at[placed].add(product, mode='drop')  34.7 us
    dot_general x6, matrix products, contribute(): jnp.einsum('tij,tjf->tif', chosen, needed, preferred_element_type=jnp.flo...  25.8 us
    gather x12, local copies, waits for them, and re-layouts, contribute(): needed = jnp.take(column_blocks, jnp.take(pool_cols, picked), axis=0)  25.5 us
    unnamed x1, blocking collectives  5.64 us
  transfers between devices with their start and end apart: 4, of which 4 were waited for; matrix products, arithmetic and copies ran while one was open for 0% of the time, Pallas kernels for 0%

commit v1 on v0

v1 whole, which is shorter than its diff:
```python
import functools
import math

import jax
import jax.numpy as jnp
from jax import lax
from jax.experimental import pallas as pl
from jax.experimental.pallas import tpu as pltpu
from jax.sharding import PartitionSpec as P

ITERS = 2
RETAIN = 0.9
RESTART = 0.1
MESH = pl.DeviceIdType.MESH
F32 = jnp.float32
BF16 = jnp.bfloat16


def kernel(
    nz, ny, nx, chunk,
    feat_ref, tiles_ref, rows_ref, cols_ref, count_ref,
    out_ref,
    pos, wout, wd, dsend, drecv, scale,
    zbuf, csend, crecv, keep_c, ysend, yrecv, keep_y, xsend, xrecv, keep_x,
    w_ss, w_rs, d_ss, d_rs, z_ss, z_rs, c_ss, c_rs, y_ss, y_rs, x_ss, x_rs,
):
    row, col = lax.axis_index("row"), lax.axis_index("col")
    z, y, x, core = row // ny, row % ny, col // 2, col % 2
    ncol = nx * 2
    shard, width = feat_ref.shape
    cap, bt = tiles_ref.shape[0], tiles_ref.shape[1]
    chunks = width // chunk
    jobs = ITERS * chunks
    col_tiles = nz * ny

    def z_peer(d):
        return (lax.rem(z + d, nz) * ny + y, col)

    def y_peer(d):
        return (z * ny + lax.rem(y + d, ny), col)

    def col_peer(d):
        return (row, lax.rem(col + d, ncol))

    def x_peer(d):
        return (row, lax.rem(x + d, nx) * 2 + core)

    sibling = (row, x * 2 + 1 - core)

    def remote(src, dst, ss, rs, device):
        return pltpu.make_async_remote_copy(
            src_ref=src, dst_ref=dst, send_sem=ss, recv_sem=rs, device_id=device, device_id_type=MESH
        )

    def z_copy(it, k, d, owner):
        j = it * chunks + k
        return remote(
            zbuf.at[it, k, owner], zbuf.at[it, k, owner], z_ss.at[j, d - 1], z_rs.at[j, d - 1], z_peer(d)
        )

    def c_copy(j):
        return remote(csend.at[j], crecv.at[j], c_ss.at[j], c_rs.at[j], sibling)

    def y_copy(j, d):
        return remote(ysend.at[j, d - 1], yrecv.at[j, d - 1], y_ss.at[j, d - 1], y_rs.at[j, d - 1], y_peer(d))

    def x_copy(j, d):
        return remote(xsend.at[j, d - 1], xrecv.at[j, d - 1], x_ss.at[j, d - 1], x_rs.at[j, d - 1], x_peer(d))

    def w_copy(d, slot):
        return remote(wout.at[lax.rem(y + d, ny)], wd.at[slot], w_ss.at[d - 1], w_rs.at[d - 1], y_peer(d))

    def d_copy(d):
        return remote(dsend.at[lax.rem(col + d, ncol)], drecv.at[d - 1], d_ss.at[d - 1], d_rs.at[d - 1], col_peer(d))

    barrier = pltpu.get_barrier_semaphore()
    peers = (
        [z_peer(d) for d in range(1, nz)]
        + [y_peer(d) for d in range(1, ny)]
        + [col_peer(d) for d in range(1, ncol)]
    )
    for device in peers:
        pl.semaphore_signal(barrier, inc=1, device_id=device, device_id_type=MESH)

    def lanes(k):
        return pl.ds(pl.multiple_of(k * chunk, chunk), chunk)

    def stage_features(k, carry):
        zbuf[0, k, z] = feat_ref[:, lanes(k)]
        return carry

    lax.fori_loop(0, chunks, stage_features, 0)
    pl.semaphore_wait(barrier, len(peers))

    def send_features(k, carry):
        for d in range(1, nz):
            z_copy(0, k, d, z).start()
        return carry

    lax.fori_loop(0, chunks, send_features, 0)

    count = count_ref[0]
    for t in range(cap):
        pos[t] = jnp.where(t < count, rows_ref[t] * col_tiles + cols_ref[t], -1)

    def place(p, carry):
        slot = jnp.int32(-1)
        for t in range(cap):
            slot = jnp.where(pos[t] == p, jnp.int32(t), slot)
        tile = tiles_ref[jnp.maximum(slot, 0)]
        tile = jnp.where(slot >= 0, tile.astype(F32), 0.0).astype(BF16)
        i, c = p // col_tiles, p % col_tiles
        wout[c % ny, i % 2, c // ny, pl.ds(pl.multiple_of((i // 2) * bt, bt), bt), :] = tile
        return carry

    lax.fori_loop(0, ncol * col_tiles, place, 0)
    for d in range(1, ny):
        w_copy(d, y).start()

    ones = jnp.ones((bt, 128), BF16)

    def row_sum(i, carry):
        total = jnp.zeros((bt, 128), F32)
        for a in range(ny):
            for b in range(nz):
                part = wout[a, i % 2, b, pl.ds(pl.multiple_of((i // 2) * bt, bt), bt), :]
                total += jnp.dot(part, ones, preferred_element_type=F32)
        dsend[i] = total
        return carry

    lax.fori_loop(0, ncol, row_sum, 0)
    for d in range(1, ncol):
        d_copy(d).start()
    wd[y] = wout[y]
    for d in range(1, ny):
        w_copy(d, lax.rem(y - d + ny, ny)).wait_recv()

    def product(it, k, source_y, half):
        total = jnp.zeros((nx * bt, chunk), F32)
        for b in range(nz):
            total += jnp.dot(wd[source_y, half, b], zbuf[it, k, b], preferred_element_type=F32)
        return total.reshape(nx, bt, chunk)

    def multiply(j):
        it, k = j // chunks, j % chunks
        for d in range(1, nz):
            z_copy(it, k, d, lax.rem(z - d + nz, nz)).wait_recv()
        for a in range(ny):
            csend[j, a] = product(it, k, a, 1 - core).astype(BF16)
        c_copy(j).start()
        for a in range(ny):
            keep_c[j % 2, a] = product(it, k, a, core)

    def over_core(j):
        c_copy(j).wait_recv()
        for d in range(1, ny):
            a = lax.rem(y + d, ny)
            ysend[j, d - 1] = (keep_c[j % 2, a] + crecv[j, a].astype(F32)).astype(BF16)
            y_copy(j, d).start()
        keep_y[j % 2] = keep_c[j % 2, y] + crecv[j, y].astype(F32)

    def over_y(j):
        for d in range(1, ny):
            y_copy(j, d).wait_recv()
        for d in range(nx):
            a = lax.rem(x + d, nx)
            total = keep_y[j % 2, a]
            for e in range(1, ny):
                total += yrecv[j, e - 1, a].astype(F32)
            if d == 0:
                keep_x[j % 2] = total
            else:
                xsend[j, d - 1] = total.astype(BF16)
                x_copy(j, d).start()

    def over_x(j):
        it, k = j // chunks, j % chunks

        @pl.when(j == 0)
        def _():
            degree = 1.0 + dsend[col]
            for d in range(1, ncol):
                d_copy(d).wait_recv()
                degree += drecv[d - 1]
            for a in range(chunk // 128):
                scale[:, a * 128:(a + 1) * 128] = RETAIN / degree

        for d in range(1, nx):
            x_copy(j, d).wait_recv()
        total = keep_x[j % 2]
        for d in range(1, nx):
            total += xrecv[j, d - 1].astype(F32)
        source = feat_ref[:, lanes(k)].astype(F32)
        fresh = ((total + zbuf[it, k, z].astype(F32)) * scale[...] + RESTART * source).astype(BF16)

        @pl.when(it == ITERS - 1)
        def _():
            out_ref[:, lanes(k)] = fresh

        @pl.when(it < ITERS - 1)
        def _():
            zbuf[it + 1, k, z] = fresh
            for d in range(1, nz):
                z_copy(it + 1, k, d, z).start()

    def step(s, carry):
        for lag, stage in ((3, over_x), (2, over_y), (1, over_core), (0, multiply)):
            j = s - lag

            @pl.when(jnp.logical_and(j >= 0, j < jobs))
            def _(stage=stage, j=j):
                stage(j)
        return carry

    lax.fori_loop(0, jobs + 3, step, 0)

    def drain(j, carry):
        it, k = j // chunks, j % chunks
        for d in range(1, nz):
            z_copy(it, k, d, z).wait_send()
        c_copy(j).wait_send()
        for d in range(1, ny):
            y_copy(j, d).wait_send()
        for d in range(1, nx):
            x_copy(j, d).wait_send()
        return carry

    lax.fori_loop(0, jobs, drain, 0)
    for d in range(1, ny):
        w_copy(d, y).wait_send()
    for d in range(1, ncol):
        d_copy(d).wait_send()


def body(nz, ny, nx, chunk, features, tile_values, tile_rows, tile_cols, tile_count):
    shard, width = features.shape
    cap, bt = tile_values.shape[2], tile_values.shape[3]
    ncol = nx * 2
    jobs = ITERS * (width // chunk)
    chunks = width // chunk
    dma = pltpu.SemaphoreType.DMA
    smem = pl.BlockSpec(memory_space=pltpu.SMEM)
    vmem = pl.BlockSpec(memory_space=pltpu.VMEM)
    return pl.pallas_call(
        functools.partial(kernel, nz, ny, nx, chunk),
        out_shape=jax.ShapeDtypeStruct((shard, width), BF16),
        in_specs=[vmem, vmem, smem, smem, smem],
        out_specs=vmem,
        scratch_shapes=[
            pltpu.SMEM((cap,), jnp.int32),
            pltpu.VMEM((ny, 2, nz, nx * bt, bt), BF16),
            pltpu.VMEM((ny, 2, nz, nx * bt, bt), BF16),
            pltpu.VMEM((ncol, bt, 128), F32),
            pltpu.VMEM((ncol - 1, bt, 128), F32),
            pltpu.VMEM((bt, chunk), F32),
            pltpu.VMEM((ITERS, chunks, nz, bt, chunk), BF16),
            pltpu.VMEM((jobs, ny, nx, bt, chunk), BF16),
            pltpu.VMEM((jobs, ny, nx, bt, chunk), BF16),
            pltpu.VMEM((2, ny, nx, bt, chunk), F32),
            pltpu.VMEM((jobs, ny - 1, nx, bt, chunk), BF16),
            pltpu.VMEM((jobs, ny - 1, nx, bt, chunk), BF16),
            pltpu.VMEM((2, nx, bt, chunk), F32),
            pltpu.VMEM((jobs, nx - 1, bt, chunk), BF16),
            pltpu.VMEM((jobs, nx - 1, bt, chunk), BF16),
            pltpu.VMEM((2, bt, chunk), F32),
            dma((ny - 1,)), dma((ny - 1,)),
            dma((ncol - 1,)), dma((ncol - 1,)),
            dma((jobs, nz - 1)), dma((jobs, nz - 1)),
            dma((jobs,)), dma((jobs,)),
            dma((jobs, ny - 1)), dma((jobs, ny - 1)),
            dma((jobs, nx - 1)), dma((jobs, nx - 1)),
        ],
        compiler_params=pltpu.CompilerParams(
            collective_id=0, has_side_effects=True, vmem_limit_bytes=62 * 1024 * 1024
        ),
    )(
        features,
        tile_values.reshape(cap, bt, bt),
        tile_rows.reshape(cap),
        tile_cols.reshape(cap),
        tile_count.reshape(1),
    )


def solution(mesh):
    n_row, n_col = mesh.shape["row"], mesh.shape["col"]
    ny = math.isqrt(n_row // 2)
    return jax.shard_map(
        functools.partial(body, n_row // ny, ny, n_col // 2, 128),
        mesh=mesh,
        in_specs=(
            P(("row", "col"), None),
            P("row", "col", None, None, None),
            P("row", "col", None),
            P("row", "col", None),
            P("row", "col"),
        ),
        out_specs=P(("row", "col"), None),
        check_vma=False,
    )
```

time: 271 us -> 83.7 us (0.31)
  waiting for transfers between devices: 144 us -> 0 us
  Pallas kernels: 0 us -> 81.2 us
  other arithmetic: 45.2 us -> 0 us
  local copies, waits for them, and re-layouts: 34.1 us -> 1.67 us
  matrix products: 25.9 us -> 0 us
  between operations: 14.5 us -> 0.66 us
  blocking collectives: 5.64 us -> 0 us
    all_gather x2 -> x0, waiting for transfers between devices: 104 us -> none  [body(): gathered = lax.all_gather(current, 'row', axis=0, tiled=True)]
    pallas_call x0 -> x1, Pallas kernels: none -> 81.2 us  [body(): pl.pallas_call(functools.partial(kernel, nz, ny, nx, chunk), out_shape=ja...]
    reduce_scatter x2 -> x0, waiting for transfers between devices: 38.9 us -> none  [body(): lax.psum_scatter(partial_value.reshape(block_rows * tile_size, feature_wi...]
    scatter-add x6 -> x0, other arithmetic: 34.7 us -> none  [own_turn(): return total.at[placed].add(product, mode='drop')]
    gather x24 -> x0, local copies, waits for them, and re-layouts: 33 us -> none  [the longest x12 25.5 us: contribute(): needed = jnp.take(column_blocks, jnp.take(pool_cols, picked), axis=0)]
    dot_general x7 -> x0, matrix products: 25.9 us -> none  [the longest x6 25.8 us: contribute(): jnp.einsum('tij,tjf->tif', chosen, needed, preferred_element_type=jnp.flo...]
    convert_element_type x4 -> x0, other arithmetic: 5.94 us -> none  [the longest x2 3.69 us: body(): current = (retain_share * (summed + current.astype(jnp.float32)) / degree...]
    unnamed x1 -> x0, blocking collectives: 5.64 us -> none
  transfers between devices with their start and end apart: 4 -> 0, of which waited for: 4 -> 0; matrix products, arithmetic and copies ran while one was open for 0% -> 0% of each run, Pallas kernels for 0% -> 0%
where the time goes in v1:
time: 83.7 us; the launch traced here: 83.5 us
  Pallas kernels  81.2 us (97%)
  local copies, waits for them, and re-layouts  1.67 us (2%)
    pallas_call x1, Pallas kernels, body(): pl.pallas_call(functools.partial(kernel, nz, ny, nx, chunk), out_shape=ja...  81.2 us

profile of v1, /device:TPU:0, one launch (start us, length us, event | category | flops | bytes accessed | tf_op | source)
XLA Modules:
  0.0 83.5 jit_solution(8375665778414625891)
XLA Ops:
  0.7 81.2 %shard_map.55 = bf16[128,1024]{1,0:T(8,128)(2,1)} custom-call(bf16[128,1024]{1,0:T(8,128)(2,1)} %feat_ref.1, bf16[24,128,128]{2,1,0:T(8,128)(2,1)} %bitcast.5, s32[24]{0:T(128)} %bitcast.6, s32[24]{0:T(128)} %bitcast.7, s32[1]{0:T(128)} %bitcast.4.count_ref), custom_call_target="tpu_custom_call" | custom-call | tf_op jit(solution)/shard_map/pallas_call | solution.py:244
  81.8 1.7 %copy.8 = bf16[128,1024]{1,0:T(8,128)(2,1)} copy(bf16[128,1024]{1,0:T(8,128)(2,1)} %shard_map.55) | data formatting | bytes 524288

commit v2 on v1

--- a/solution.py
+++ b/solution.py
@@ -110,21 +110,21 @@
         tile = tiles_ref[jnp.maximum(slot, 0)]
         tile = jnp.where(slot >= 0, tile.astype(F32), 0.0).astype(BF16)
         i, c = p // col_tiles, p % col_tiles
-        wout[c % ny, i % 2, c // ny, pl.ds(pl.multiple_of((i // 2) * bt, bt), bt), :] = tile
+        rows = pl.ds(pl.multiple_of((i // 2) * bt, bt), bt)
+        wout[c % ny, i % 2, rows, pl.ds(pl.multiple_of((c // ny) * bt, bt), bt)] = tile
         return carry
 
     lax.fori_loop(0, ncol * col_tiles, place, 0)
     for d in range(1, ny):
         w_copy(d, y).start()
 
-    ones = jnp.ones((bt, 128), BF16)
+    ones = jnp.ones((nz * bt, 128), BF16)
 
     def row_sum(i, carry):
         total = jnp.zeros((bt, 128), F32)
         for a in range(ny):
-            for b in range(nz):
-                part = wout[a, i % 2, b, pl.ds(pl.multiple_of((i // 2) * bt, bt), bt), :]
-                total += jnp.dot(part, ones, preferred_element_type=F32)
+            part = wout[a, i % 2, pl.ds(pl.multiple_of((i // 2) * bt, bt), bt), :]
+            total += jnp.dot(part, ones, preferred_element_type=F32)
         dsend[i] = total
         return carry
 
@@ -136,9 +136,8 @@
         w_copy(d, lax.rem(y - d + ny, ny)).wait_recv()
 
     def product(it, k, source_y, half):
-        total = jnp.zeros((nx * bt, chunk), F32)
-        for b in range(nz):
-            total += jnp.dot(wd[source_y, half, b], zbuf[it, k, b], preferred_element_type=F32)
+        blocks = zbuf[it, k].reshape(nz * bt, chunk)
+        total = jnp.dot(wd[source_y, half], blocks, preferred_element_type=F32)
         return total.reshape(nx, bt, chunk)
 
     def multiply(j):
@@ -146,34 +145,34 @@
         for d in range(1, nz):
             z_copy(it, k, d, lax.rem(z - d + nz, nz)).wait_recv()
         for a in range(ny):
-            csend[j, a] = product(it, k, a, 1 - core).astype(BF16)
+            csend[j, :, a] = product(it, k, a, 1 - core).astype(BF16)
         c_copy(j).start()
         for a in range(ny):
-            keep_c[j % 2, a] = product(it, k, a, core)
+            keep_c[j % 2, :, a] = product(it, k, a, core)
 
     def over_core(j):
         c_copy(j).wait_recv()
-        for d in range(1, ny):
+        for d in range(1, nx):
+            a = lax.rem(x + d, nx)
+            xsend[j, d - 1] = (keep_c[j % 2, a] + crecv[j, a].astype(F32)).astype(BF16)
+            x_copy(j, d).start()
+        keep_x[j % 2] = keep_c[j % 2, x] + crecv[j, x].astype(F32)
+
+    def over_x(j):
+        for d in range(1, nx):
+            x_copy(j, d).wait_recv()
+        for d in range(ny):
             a = lax.rem(y + d, ny)
-            ysend[j, d - 1] = (keep_c[j % 2, a] + crecv[j, a].astype(F32)).astype(BF16)
-            y_copy(j, d).start()
-        keep_y[j % 2] = keep_c[j % 2, y] + crecv[j, y].astype(F32)
+            total = keep_x[j % 2, a]
+            for e in range(1, nx):
+                total += xrecv[j, e - 1, a].astype(F32)
+            if d == 0:
+                keep_y[j % 2] = total
+            else:
+                ysend[j, d - 1] = total.astype(BF16)
+                y_copy(j, d).start()
 
     def over_y(j):
-        for d in range(1, ny):
-            y_copy(j, d).wait_recv()
-        for d in range(nx):
-            a = lax.rem(x + d, nx)
-            total = keep_y[j % 2, a]
-            for e in range(1, ny):
-                total += yrecv[j, e - 1, a].astype(F32)
-            if d == 0:
-                keep_x[j % 2] = total
-            else:
-                xsend[j, d - 1] = total.astype(BF16)
-                x_copy(j, d).start()
-
-    def over_x(j):
         it, k = j // chunks, j % chunks
 
         @pl.when(j == 0)
@@ -185,11 +184,11 @@
             for a in range(chunk // 128):
                 scale[:, a * 128:(a + 1) * 128] = RETAIN / degree
 
-        for d in range(1, nx):
-            x_copy(j, d).wait_recv()
-        total = keep_x[j % 2]
-        for d in range(1, nx):
-            total += xrecv[j, d - 1].astype(F32)
+        for d in range(1, ny):
+            y_copy(j, d).wait_recv()
+        total = keep_y[j % 2]
+        for d in range(1, ny):
+            total += yrecv[j, d - 1].astype(F32)
         source = feat_ref[:, lanes(k)].astype(F32)
         fresh = ((total + zbuf[it, k, z].astype(F32)) * scale[...] + RESTART * source).astype(BF16)
 
@@ -204,7 +203,7 @@
                 z_copy(it + 1, k, d, z).start()
 
     def step(s, carry):
-        for lag, stage in ((3, over_x), (2, over_y), (1, over_core), (0, multiply)):
+        for lag, stage in ((3, over_y), (2, over_x), (1, over_core), (0, multiply)):
             j = s - lag
 
             @pl.when(jnp.logical_and(j >= 0, j < jobs))
@@ -248,21 +247,21 @@
         out_specs=vmem,
         scratch_shapes=[
             pltpu.SMEM((cap,), jnp.int32),
-            pltpu.VMEM((ny, 2, nz, nx * bt, bt), BF16),
-            pltpu.VMEM((ny, 2, nz, nx * bt, bt), BF16),
+            pltpu.VMEM((ny, 2, nx * bt, nz * bt), BF16),
+            pltpu.VMEM((ny, 2, nx * bt, nz * bt), BF16),
             pltpu.VMEM((ncol, bt, 128), F32),
             pltpu.VMEM((ncol - 1, bt, 128), F32),
             pltpu.VMEM((bt, chunk), F32),
             pltpu.VMEM((ITERS, chunks, nz, bt, chunk), BF16),
-            pltpu.VMEM((jobs, ny, nx, bt, chunk), BF16),
-            pltpu.VMEM((jobs, ny, nx, bt, chunk), BF16),
-            pltpu.VMEM((2, ny, nx, bt, chunk), F32),
-            pltpu.VMEM((jobs, ny - 1, nx, bt, chunk), BF16),
-            pltpu.VMEM((jobs, ny - 1, nx, bt, chunk), BF16),
-            pltpu.VMEM((2, nx, bt, chunk), F32),
-            pltpu.VMEM((jobs, nx - 1, bt, chunk), BF16),
-            pltpu.VMEM((jobs, nx - 1, bt, chunk), BF16),
+            pltpu.VMEM((jobs, nx, ny, bt, chunk), BF16),
+            pltpu.VMEM((jobs, nx, ny, bt, chunk), BF16),
+            pltpu.VMEM((2, nx, ny, bt, chunk), F32),
+            pltpu.VMEM((jobs, ny - 1, bt, chunk), BF16),
+            pltpu.VMEM((jobs, ny - 1, bt, chunk), BF16),
             pltpu.VMEM((2, bt, chunk), F32),
+            pltpu.VMEM((jobs, nx - 1, ny, bt, chunk), BF16),
+            pltpu.VMEM((jobs, nx - 1, ny, bt, chunk), BF16),
+            pltpu.VMEM((2, ny, bt, chunk), F32),
             dma((ny - 1,)), dma((ny - 1,)),
             dma((ncol - 1,)), dma((ncol - 1,)),
             dma((jobs, nz - 1)), dma((jobs, nz - 1)),
@@ -286,7 +285,7 @@
     n_row, n_col = mesh.shape["row"], mesh.shape["col"]
     ny = math.isqrt(n_row // 2)
     return jax.shard_map(
-        functools.partial(body, n_row // ny, ny, n_col // 2, 128),
+        functools.partial(body, n_row // ny, ny, n_col // 2, 256),
         mesh=mesh,
         in_specs=(
             P(("row", "col"), None),

time: 83.7 us -> 69.3 us (0.83)
  the two profiles are of different devices: /device:TPU:0 before, /device:TPU:26 now
where the time goes in v2:
time: 69.3 us; the launch traced here: 69.1 us
  Pallas kernels  66.8 us (96%)
  local copies, waits for them, and re-layouts  1.67 us (2%)
    pallas_call x1, Pallas kernels, body(): pl.pallas_call(functools.partial(kernel, nz, ny, nx, chunk), out_shape=ja...  66.8 us
    unnamed x1, local copies, waits for them, and re-layouts  1.67 us

profile of v2, /device:TPU:26, one launch (start us, length us, event | category | flops | bytes accessed | tf_op | source)
XLA Modules:
  0.0 69.1 jit_solution(11874110604724466360)
XLA Ops:
  0.7 66.8 %shard_map.55 = bf16[128,1024]{1,0:T(8,128)(2,1)} custom-call(bf16[128,1024]{1,0:T(8,128)(2,1)} %feat_ref.1, bf16[24,128,128]{2,1,0:T(8,128)(2,1)} %bitcast.5, s32[24]{0:T(128)} %bitcast.6, s32[24]{0:T(128)} %bitcast.7, s32[1]{0:T(128)} %bitcast.4.count_ref), custom_call_target="tpu_custom_call" | custom-call | tf_op jit(solution)/shard_map/pallas_call | solution.py:243
  67.4 1.7 %copy.8 = bf16[128,1024]{1,0:T(8,128)(2,1)} copy(bf16[128,1024]{1,0:T(8,128)(2,1)} %shard_map.55) | data formatting | bytes 524288

commit v3 on v2

--- a/solution.py
+++ b/solution.py
@@ -93,7 +93,7 @@
     pl.semaphore_wait(barrier, len(peers))
 
     def send_features(k, carry):
-        for d in range(1, nz):
+        for d in range(nz - 1, 0, -1):
             z_copy(0, k, d, z).start()
         return carry
 

time: 69.3 us -> 67.8 us (0.978)
  the two profiles are of different devices: /device:TPU:26 before, /device:TPU:0 now
where the time goes in v3:
time: 67.8 us; the launch traced here: 67 us
  Pallas kernels  64.6 us (95%)
  local copies, waits for them, and re-layouts  1.67 us (2%)
    pallas_call x1, Pallas kernels, body(): pl.pallas_call(functools.partial(kernel, nz, ny, nx, chunk), out_shape=ja...  64.6 us
    unnamed x1, local copies, waits for them, and re-layouts  1.67 us

profile of v3, /device:TPU:0, one launch (start us, length us, event | category | flops | bytes accessed | tf_op | source)
XLA Modules:
  0.0 67.0 jit_solution(6339521609108141869)
XLA Ops:
  0.7 64.6 %shard_map.55 = bf16[128,1024]{1,0:T(8,128)(2,1)} custom-call(bf16[128,1024]{1,0:T(8,128)(2,1)} %feat_ref.1, bf16[24,128,128]{2,1,0:T(8,128)(2,1)} %bitcast.5, s32[24]{0:T(128)} %bitcast.6, s32[24]{0:T(128)} %bitcast.7, s32[1]{0:T(128)} %bitcast.4.count_ref), custom_call_target="tpu_custom_call" | custom-call | tf_op jit(solution)/shard_map/pallas_call | solution.py:243
  65.3 1.7 %copy.8 = bf16[128,1024]{1,0:T(8,128)(2,1)} copy(bf16[128,1024]{1,0:T(8,128)(2,1)} %shard_map.55) | data formatting | bytes 524288

commit v4 on v3

--- a/solution.py
+++ b/solution.py
@@ -103,20 +103,22 @@
     for t in range(cap):
         pos[t] = jnp.where(t < count, rows_ref[t] * col_tiles + cols_ref[t], -1)
 
-    def place(p, carry):
+    def place(d, q, carry):
+        i, c = q // nz, (q % nz) * ny + lax.rem(y + d, ny)
+        p = i * col_tiles + c
         slot = jnp.int32(-1)
         for t in range(cap):
             slot = jnp.where(pos[t] == p, jnp.int32(t), slot)
         tile = tiles_ref[jnp.maximum(slot, 0)]
         tile = jnp.where(slot >= 0, tile.astype(F32), 0.0).astype(BF16)
-        i, c = p // col_tiles, p % col_tiles
         rows = pl.ds(pl.multiple_of((i // 2) * bt, bt), bt)
         wout[c % ny, i % 2, rows, pl.ds(pl.multiple_of((c // ny) * bt, bt), bt)] = tile
         return carry
 
-    lax.fori_loop(0, ncol * col_tiles, place, 0)
     for d in range(1, ny):
+        lax.fori_loop(0, ncol * nz, functools.partial(place, d), 0)
         w_copy(d, y).start()
+    lax.fori_loop(0, ncol * nz, functools.partial(place, 0), 0)
 
     ones = jnp.ones((nz * bt, 128), BF16)
 

time: 67.8 us -> 67.5 us (level)
  no operation moved by 1% of the time
where the time goes in v4:
time: 67.5 us; the launch traced here: 66.7 us
  Pallas kernels  64.3 us (95%)
  local copies, waits for them, and re-layouts  1.67 us (2%)
    pallas_call x1, Pallas kernels, body(): pl.pallas_call(functools.partial(kernel, nz, ny, nx, chunk), out_shape=ja...  64.3 us
    unnamed x1, local copies, waits for them, and re-layouts  1.67 us

profile of v4, /device:TPU:0, one launch (start us, length us, event | category | flops | bytes accessed | tf_op | source)
XLA Modules:
  0.0 66.7 jit_solution(3112583294692737476)
XLA Ops:
  0.7 64.3 %shard_map.55 = bf16[128,1024]{1,0:T(8,128)(2,1)} custom-call(bf16[128,1024]{1,0:T(8,128)(2,1)} %feat_ref.1, bf16[24,128,128]{2,1,0:T(8,128)(2,1)} %bitcast.5, s32[24]{0:T(128)} %bitcast.6, s32[24]{0:T(128)} %bitcast.7, s32[1]{0:T(128)} %bitcast.4.count_ref), custom_call_target="tpu_custom_call" | custom-call | tf_op jit(solution)/shard_map/pallas_call | solution.py:245
  65.0 1.7 %copy.8 = bf16[128,1024]{1,0:T(8,128)(2,1)} copy(bf16[128,1024]{1,0:T(8,128)(2,1)} %shard_map.55) | data formatting | bytes 524288
